TPU v7x, 32 devices: a whole 2x2x4 slice. The times are simulated.
32 devices in a mesh: shot: 2 (over y), slab: 8 (over z, x), side: 2 (over core).
Axes of the slice: x: 2, y: 2, z: 4, core: 2. Of those that a mesh axis runs over, the one named last changes fastest.
Arguments:
- field_now: float32 [256, 64, 128], P(('shot', 'slab'), 'side'), parts along dimension 0, may hold values from -6 to 6
- field_before: float32 [256, 64, 128], P(('shot', 'slab'), 'side'), parts along dimension 0, may hold values from -6 to 6
- courant: float32 [256, 64, 128], P(('shot', 'slab'), 'side'), parts along dimension 0, may hold values from 0.05 to 0.19
- wavelet: float32 [8], P('shot'), parts along dimension 0, may hold values from -60 to 60
- source_cell: int32 [2], P('shot'), parts along dimension 0, may hold values from 0 to 524287
- traces: float32 [8, 512], P('shot'), parts along dimension 0, may hold values from -60 to 60
- receiver_cells: int32 [1024], P('shot'), parts along dimension 0, may hold values from 0 to 524287
- offsets: int32 [64], P('shot'), parts along dimension 0, may hold values from 0 to 31, each once
Outputs:
- now_out: float32 [256, 64, 128], P(('shot', 'slab'), 'side'), parts along dimension 0
- before_out: float32 [256, 64, 128], P(('shot', 'slab'), 'side'), parts along dimension 0
- image: bfloat16 [256, 16, 64, 128], P(('shot', 'slab'), None, 'side'), parts along dimension 0
There are 2 independent parts, one for each index of `shot`. A program takes and returns all parts, laid end to end along the dimension named above; each array names one. Nothing has to cross between parts.
Inputs may be any that keep to these rules, and one draw needn't show every extreme that they name: `offsets`: each value occurs exactly once.
All inputs are finite; a program needn't handle non-finite values.
Results may differ from a plain program's by a relative error of at most 0.001.
Values sent between devices are 32-bit elements; how exact they have to be, the bound alone decides.
A program may use at most 64 MiB of HBM per device.

v0:
```python
import jax
import jax.numpy as jnp
from jax import lax
from jax.sharding import PartitionSpec as P

LAGS = 32
STEPS = 4
NIMG = 2


STENCIL_WEIGHTS = (-205.0 / 72.0, 8.0 / 5.0, -1.0 / 5.0, 8.0 / 315.0, -1.0 / 560.0)


def extended(block, sides, width, periodic):
    for axis, dim in sides:
        count = lax.axis_size(axis)
        forward = [(i, i + 1) for i in range(count - 1)]
        if periodic:
            forward.append((count - 1, 0))
        backward = [(target, source) for source, target in forward]
        low = lax.ppermute(
            lax.slice_in_dim(block, block.shape[dim] - width, None, axis=dim), axis, forward
        )
        high = lax.ppermute(lax.slice_in_dim(block, 0, width, axis=dim), axis, backward)
        block = jnp.concatenate([low, block, high], axis=dim)
    return block


def from_behind(value, axis, steps):
    count = lax.axis_size(axis)
    pairs = [(source, (source + steps) % count) for source in range(count)]
    return lax.ppermute(value, axis, pairs)


def stencil(padded):
    depth = padded.shape[0] - 8
    across = padded.shape[1] - 8
    along = padded.shape[2] - 8
    center = padded[4 : 4 + depth, 4 : 4 + across, 4 : 4 + along]
    summed = 3.0 * STENCIL_WEIGHTS[0] * center
    for reach in range(1, 5):
        pairs = (
            padded[4 + reach : 4 + reach + depth, 4 : 4 + across, 4 : 4 + along]
            + padded[4 - reach : 4 - reach + depth, 4 : 4 + across, 4 : 4 + along]
        )
        pairs = (
            pairs
            + padded[4 : 4 + depth, 4 + reach : 4 + reach + across, 4 : 4 + along]
            + padded[4 : 4 + depth, 4 - reach : 4 - reach + across, 4 : 4 + along]
        )
        pairs = (
            pairs
            + padded[4 : 4 + depth, 4 : 4 + across, 4 + reach : 4 + reach + along]
            + padded[4 : 4 + depth, 4 : 4 + across, 4 - reach : 4 - reach + along]
        )
        summed = summed + STENCIL_WEIGHTS[reach] * pairs
    return summed


def shards(field_now, field_before, courant, wavelet, source_cell, traces, receiver_cells, offsets):
    depth_rows, cols_dev, along_cells = field_now.shape
    quarter = lax.axis_size("slab") // 4
    half_size = 2 * quarter
    slab_place = lax.axis_index("slab")
    side_place = lax.axis_index("side")
    is_receiver = (slab_place < quarter) | (slab_place >= 3 * quarter)
    depth_start = jnp.where(
        is_receiver,
        (slab_place - 3 * quarter) % (4 * quarter) * depth_rows,
        (slab_place - quarter) * depth_rows,
    )
    col_start = side_place * cols_dev
    cols_all = cols_dev * lax.axis_size("side")

    def local_cells(cells):
        cell_depth = cells // (cols_all * along_cells) - depth_start
        cell_across = cells // along_cells % cols_all - col_start
        cell_along = cells % along_cells
        inside = (
            (cell_depth >= 0)
            & (cell_depth < depth_rows)
            & (cell_across >= 0)
            & (cell_across < cols_dev)
        )
        flat = jnp.where(
            inside, (cell_depth * cols_dev + cell_across) * along_cells + cell_along, 0
        )
        return (flat, inside)

    source_flat, source_inside = local_cells(source_cell)
    receiver_flat, receiver_inside = local_cells(receiver_cells)
    source_live = source_inside & jnp.logical_not(is_receiver)
    receiver_live = receiver_inside & is_receiver
    seam_low = (slab_place == quarter) | (slab_place == 3 * quarter)
    seam_high = (slab_place == quarter - 1) | (slab_place == 3 * quarter - 1)
    now = field_now
    before = field_before
    snapshots = []
    for instant in range(STEPS):
        impulse = jnp.zeros((now.size,), jnp.float32)
        impulse = impulse.at[source_flat].add(jnp.where(source_live, wavelet[instant], 0.0))
        impulse = impulse.at[receiver_flat].add(jnp.where(receiver_live, traces[instant], 0.0))
        impulse = impulse.reshape(now.shape)
        padded = extended(now, (("slab", 0), ("side", 1)), 4, True)
        row_ids = lax.broadcasted_iota(jnp.int32, padded.shape, 0)
        col_ids = lax.broadcasted_iota(jnp.int32, padded.shape, 1)
        seam = seam_low & (row_ids < 4) | seam_high & (row_ids >= depth_rows + 4)
        edge = (side_place == 0) & (col_ids < 4) | (side_place == lax.axis_size("side") - 1) & (
            col_ids >= cols_dev + 4
        )
        padded = jnp.where(seam | edge, 0.0, padded)
        padded = jnp.pad(padded, ((0, 0), (0, 0), (4, 4)))
        later = 2.0 * now - before + courant * (stencil(padded) + impulse)
        before = now
        now = later
        snapshots.append(now)
    margin = LAGS // 2
    stacked = jnp.stack(snapshots)
    picked = jnp.array([2 * j + 1 for j in range(NIMG)], jnp.int32)
    own_index = jnp.where(is_receiver, STEPS - 1 - picked, picked)
    partner_index = jnp.where(is_receiver, picked, STEPS - 1 - picked)
    own_sel = jnp.take(stacked, own_index, axis=0)
    partner_stack = from_behind(stacked, "slab", half_size)
    partner_sel = jnp.take(partner_stack, partner_index, axis=0)
    source_sel = jnp.where(is_receiver, partner_sel, own_sel)
    receiver_sel = jnp.where(is_receiver, own_sel, partner_sel)
    paired = jnp.stack([source_sel, receiver_sel])
    widened = extended(paired, (("side", 3),), margin, False)
    wide_source = widened[0]
    wide_receiver = widened[1]
    slot_base = jnp.where(is_receiver, margin, 0)
    slots = []
    for lag_slot in range(margin):
        offset_now = (
            lax.dynamic_index_in_dim(offsets, slot_base + lag_slot, 0, keepdims=False) - margin
        )
        s_piece = lax.dynamic_slice_in_dim(wide_source, margin - offset_now, cols_dev, 2)
        r_piece = lax.dynamic_slice_in_dim(wide_receiver, margin + offset_now, cols_dev, 2)
        slots.append(jnp.sum(s_piece * r_piece, axis=0).astype(jnp.bfloat16))
    image = jnp.stack(slots, axis=1)
    return (now, before, image)


def solution(mesh):
    return jax.shard_map(
        shards,
        mesh=mesh,
        in_specs=(
            P(("shot", "slab"), "side", None),
            P(("shot", "slab"), "side", None),
            P(("shot", "slab"), "side", None),
            P("shot"),
            P("shot"),
            P("shot", None),
            P("shot"),
            P("shot"),
        ),
        out_specs=(
            P(("shot", "slab"), "side", None),
            P(("shot", "slab"), "side", None),
            P(("shot", "slab"), None, "side", None),
        ),
        check_vma=False,
    )
```

profile of v0, /device:TPU:1, one launch (start us, length us, event | category | flops | bytes accessed | tf_op | source)
XLA Modules:
  0.0 160.3 jit_solution(3012491340662920826)
XLA Ops:
  0.6 0.9 fusion.92
  1.5 5.1 %collective-permute-start.1 = (f32[4,32,128]{2,1,0:T(8,128)S(1)}, f32[4,32,128]{2,1,0:T(8,128)S(1)}, u32[]{:S(2)}, u32[]{:S(2)}) collective-permute-start(f32[4,32,128]{2,1,0:T(8,128)S(1)} %get-tuple-element.96), channel_id=1, source_target_pairs={{2,0},{4,2},{6,4},{8,6},{10,8},{12,10},{14,12},{0,14},{3,1},{5,3},... | collective-permute-start | bytes 196616 | tf_op jit(solution)/shard_map/ppermute | solution.py:24
  10.2 1.5 select_dynamic-update-slice_fusion.3
  12.5 1.0 constant_dynamic-update-slice_fusion.1
  13.5 2.2 %collective-permute-start.2 = (f32[24,4,128]{2,1,0:T(4,128)S(1)}, f32[24,4,128]{2,1,0:T(4,128)S(1)}, u32[]{:S(2)}, u32[]{:S(2)}) collective-permute-start(f32[24,4,128]{2,1,0:T(4,128)S(1)} %get-tuple-element.88), channel_id=1, source_target_pairs={{0,1},{1,0},{2,3},{3,2},{4,5},{5,4},{6,7},{7,6},{8,9},{9,8},{10,11... | collective-permute-start | bytes 147464 | tf_op jit(solution)/shard_map/ppermute | solution.py:21
  15.8 3.9 %scatter_fusion = f32[65536]{0:T(1024)S(1)} fusion(f32[65536]{0:T(1024)S(1)} %select_dynamic-update-slice_fusion.3, s32[512]{0:T(512)S(1)} %compare_select_fusion, f32[512]{0:T(512)S(1)} %get-tuple-element.72), kind=kCustom, calls=%fused_computation.2 | custom fusion | flops 512 | bytes 8192 | tf_op jit(solution)/shard_map/scatter-add | solution.py:102
  20.6 4.1 %collective-permute-start.5 = (f32[4,32,128]{2,1,0:T(8,128)S(1)}, f32[4,32,128]{2,1,0:T(8,128)S(1)}, u32[]{:S(2)}, u32[]{:S(2)}) collective-permute-start(f32[4,32,128]{2,1,0:T(8,128)S(1)} %get-tuple-element.95), channel_id=1, source_target_pairs={{2,0},{4,2},{6,4},{8,6},{10,8},{12,10},{14,12},{0,14},{3,1},{5,3},... | collective-permute-start | bytes 196616 | tf_op jit(solution)/shard_map/ppermute | solution.py:24
  24.8 1.6 %collective-permute-done.4 = f32[4,32,128]{2,1,0:T(8,128)S(1)} collective-permute-done((f32[4,32,128]{2,1,0:T(8,128)S(1)}, f32[4,32,128]{2,1,0:T(8,128)S(1)}, u32[]{:S(2)}, u32[]{:S(2)}) %collective-permute-start.4) | collective-permute-done | bytes 65568 | tf_op jit(solution)/shard_map/ppermute | solution.py:21
  26.5 1.6 collective-permute-start.6
  29.0 3.9 %scatter_fusion.1 = f32[65536]{0:T(1024)S(1)} fusion(f32[65536]{0:T(1024)S(1)} %select_dynamic-update-slice_fusion.2, s32[512]{0:T(512)S(1)} %compare_select_fusion, f32[512]{0:T(512)S(1)} %get-tuple-element.120), kind=kCustom, calls=%fused_computation.3 | custom fusion | flops 512 | bytes 8192 | tf_op jit(solution)/shard_map/scatter-add | solution.py:102
  33.8 4.4 %collective-permute-start.9 = (f32[4,32,128]{2,1,0:T(8,128)S(1)}, f32[4,32,128]{2,1,0:T(8,128)S(1)}, u32[]{:S(2)}, u32[]{:S(2)}) collective-permute-start(f32[4,32,128]{2,1,0:T(8,128)S(1)} %get-tuple-element.93), channel_id=1, source_target_pairs={{2,0},{4,2},{6,4},{8,6},{10,8},{12,10},{14,12},{0,14},{3,1},{5,3},... | collective-permute-start | bytes 196616 | tf_op jit(solution)/shard_map/ppermute | solution.py:24
  38.3 2.0 %collective-permute-done.8 = f32[4,32,128]{2,1,0:T(8,128)S(1)} collective-permute-done((f32[4,32,128]{2,1,0:T(8,128)S(1)}, f32[4,32,128]{2,1,0:T(8,128)S(1)}, u32[]{:S(2)}, u32[]{:S(2)}) %collective-permute-start.8) | collective-permute-done | bytes 65568 | tf_op jit(solution)/shard_map/ppermute | solution.py:21
  40.3 1.0 collective-permute-start.10
  42.3 3.9 %scatter_fusion.2 = f32[65536]{0:T(1024)S(1)} fusion(f32[65536]{0:T(1024)S(1)} %select_dynamic-update-slice_fusion.1, s32[512]{0:T(512)S(1)} %compare_select_fusion, f32[512]{0:T(512)S(1)} %get-tuple-element.121), kind=kCustom, calls=%fused_computation.4 | custom fusion | flops 512 | bytes 8192 | tf_op jit(solution)/shard_map/scatter-add | solution.py:102
  47.1 4.4 %collective-permute-start.13 = (f32[4,32,128]{2,1,0:T(8,128)S(1)}, f32[4,32,128]{2,1,0:T(8,128)S(1)}, u32[]{:S(2)}, u32[]{:S(2)}) collective-permute-start(f32[4,32,128]{2,1,0:T(8,128)S(1)} %get-tuple-element.91), channel_id=1, source_target_pairs={{2,0},{4,2},{6,4},{8,6},{10,8},{12,10},{14,12},{0,14},{3,1},{5,3},... | collective-permute-start | bytes 196616 | tf_op jit(solution)/shard_map/ppermute | solution.py:24
  51.5 2.0 %collective-permute-done.12 = f32[4,32,128]{2,1,0:T(8,128)S(1)} collective-permute-done((f32[4,32,128]{2,1,0:T(8,128)S(1)}, f32[4,32,128]{2,1,0:T(8,128)S(1)}, u32[]{:S(2)}, u32[]{:S(2)}) %collective-permute-start.12) | collective-permute-done | bytes 65568 | tf_op jit(solution)/shard_map/ppermute | solution.py:21
  53.6 1.0 collective-permute-start.14
  55.6 3.9 %scatter_fusion.3 = f32[65536]{0:T(1024)S(1)} fusion(f32[65536]{0:T(1024)S(1)} %select_dynamic-update-slice_fusion, s32[512]{0:T(512)S(1)} %compare_select_fusion, f32[512]{0:T(512)S(1)} %get-tuple-element.122), kind=kCustom, calls=%fused_computation.5 | custom fusion | flops 512 | bytes 8192 | tf_op jit(solution)/shard_map/scatter-add | solution.py:102
  61.7 47.1 %collective-permute-done.16 = f32[4,16,32,128]{3,2,1,0:T(8,128)S(1)} collective-permute-done((f32[4,16,32,128]{3,2,1,0:T(8,128)S(1)}, f32[4,16,32,128]{3,2,1,0:T(8,128)S(1)}, u32[]{:S(2)}, u32[]{:S(2)}) %collective-permute-start.16) | collective-permute-done | bytes 1048608 | tf_op jit(solution)/shard_map/ppermute | solution.py:32
  109.7 1.3 collective-permute-start.17
  111.0 3.3 %collective-permute-start.18 = (f32[2,2,16,16,128]{4,3,2,1,0:T(8,128)S(1)}, f32[2,2,16,16,128]{4,3,2,1,0:T(8,128)S(1)}, u32[]{:S(2)}, u32[]{:S(2)}) collective-permute-start(f32[2,2,16,16,128]{4,3,2,1,0:T(8,128)S(1)} %get-tuple-element.81), channel_id=1, source_target_pairs={{1,0},{3,2},{5,4},{7,6},{9,8},{11,10},{13,12},{15,14},{17,16},{19,... | collective-permute-start | bytes 1572872 | tf_op jit(solution)/shard_map/ppermute | solution.py:24
  155.6 1.5 multiply_reduce_fusion.8
  157.3 1.4 multiply_reduce_fusion
  159.0 1.3 copy-done.7
  (99 shorter events, 13.3 us)
Async XLA Ops:
  1.5 11.9 %collective-permute-start.1 = (f32[4,32,128]{2,1,0:T(8,128)S(1)}, f32[4,32,128]{2,1,0:T(8,128)S(1)}, u32[]{:S(2)}, u32[]{:S(2)}) collective-permute-start(f32[4,32,128]{2,1,0:T(8,128)S(1)} %get-tuple-element.96), channel_id=1, source_target_pairs={{2,0},{4,2},{6,4},{8,6},{10,8},{12,10},{14,12},{0,14},{3,1},{5,3},... | collective-permute-start | bytes 196616 | tf_op jit(solution)/shard_map/ppermute | solution.py:24
  6.6 5.8 %collective-permute-start = (f32[4,32,128]{2,1,0:T(8,128)S(1)}, f32[4,32,128]{2,1,0:T(8,128)S(1)}, u32[]{:S(2)}, u32[]{:S(2)}) collective-permute-start(f32[4,32,128]{2,1,0:T(8,128)S(1)} %get-tuple-element.97), channel_id=1, source_target_pairs={{0,2},{2,4},{4,6},{6,8},{8,10},{10,12},{12,14},{14,0},{1,3},{3,5},... | collective-permute-start | bytes 196616 | tf_op jit(solution)/shard_map/ppermute | solution.py:21
  13.5 6.2 %collective-permute-start.2 = (f32[24,4,128]{2,1,0:T(4,128)S(1)}, f32[24,4,128]{2,1,0:T(4,128)S(1)}, u32[]{:S(2)}, u32[]{:S(2)}) collective-permute-start(f32[24,4,128]{2,1,0:T(4,128)S(1)} %get-tuple-element.88), channel_id=1, source_target_pairs={{0,1},{1,0},{2,3},{3,2},{4,5},{5,4},{6,7},{7,6},{8,9},{9,8},{10,11... | collective-permute-start | bytes 147464 | tf_op jit(solution)/shard_map/ppermute | solution.py:21
  15.7 4.1 %collective-permute-start.3 = (f32[24,4,128]{2,1,0:T(4,128)S(1)}, f32[24,4,128]{2,1,0:T(4,128)S(1)}, u32[]{:S(2)}, u32[]{:S(2)}) collective-permute-start(f32[24,4,128]{2,1,0:T(4,128)S(1)} %get-tuple-element.89), channel_id=1, source_target_pairs={{1,0},{0,1},{3,2},{2,3},{5,4},{4,5},{7,6},{6,7},{9,8},{8,9},{11,10... | collective-permute-start | bytes 147464 | tf_op jit(solution)/shard_map/ppermute | solution.py:24
  15.8 4.1 %copy-start.4 = (f32[16,32,128]{2,1,0:T(8,128)S(1)}, f32[16,32,128]{2,1,0:T(8,128)}, u32[]{:S(2)}) copy-start(f32[16,32,128]{2,1,0:T(8,128)} %param.20) | copy-start | bytes 786436
  19.9 8.2 %copy-start.6 = (f32[4]{0:T(128)S(1)}, f32[4]{0:T(128)}, u32[]{:S(2)}) copy-start(f32[4]{0:T(128)} %param.22) | copy-start | bytes 52
  20.6 5.9 %collective-permute-start.4 = (f32[4,32,128]{2,1,0:T(8,128)S(1)}, f32[4,32,128]{2,1,0:T(8,128)S(1)}, u32[]{:S(2)}, u32[]{:S(2)}) collective-permute-start(f32[4,32,128]{2,1,0:T(8,128)S(1)} %get-tuple-element.94), channel_id=1, source_target_pairs={{0,2},{2,4},{4,6},{6,8},{8,10},{10,12},{12,14},{14,0},{1,3},{3,5},... | collective-permute-start | bytes 196616 | tf_op jit(solution)/shard_map/ppermute | solution.py:21
  20.6 5.8 %collective-permute-start.5 = (f32[4,32,128]{2,1,0:T(8,128)S(1)}, f32[4,32,128]{2,1,0:T(8,128)S(1)}, u32[]{:S(2)}, u32[]{:S(2)}) collective-permute-start(f32[4,32,128]{2,1,0:T(8,128)S(1)} %get-tuple-element.95), channel_id=1, source_target_pairs={{2,0},{4,2},{6,4},{8,6},{10,8},{12,10},{14,12},{0,14},{3,1},{5,3},... | collective-permute-start | bytes 196616 | tf_op jit(solution)/shard_map/ppermute | solution.py:24
  26.5 6.5 %collective-permute-start.6 = (f32[24,4,128]{2,1,0:T(4,128)S(1)}, f32[24,4,128]{2,1,0:T(4,128)S(1)}, u32[]{:S(2)}, u32[]{:S(2)}) collective-permute-start(f32[24,4,128]{2,1,0:T(4,128)S(1)} %get-tuple-element.86), channel_id=1, source_target_pairs={{0,1},{1,0},{2,3},{3,2},{4,5},{5,4},{6,7},{7,6},{8,9},{9,8},{10,11... | collective-permute-start | bytes 147464 | tf_op jit(solution)/shard_map/ppermute | solution.py:21
  28.0 4.9 %collective-permute-start.7 = (f32[24,4,128]{2,1,0:T(4,128)S(1)}, f32[24,4,128]{2,1,0:T(4,128)S(1)}, u32[]{:S(2)}, u32[]{:S(2)}) collective-permute-start(f32[24,4,128]{2,1,0:T(4,128)S(1)} %get-tuple-element.87), channel_id=1, source_target_pairs={{1,0},{0,1},{3,2},{2,3},{5,4},{4,5},{7,6},{6,7},{9,8},{8,9},{11,10... | collective-permute-start | bytes 147464 | tf_op jit(solution)/shard_map/ppermute | solution.py:24
  33.8 6.5 %collective-permute-start.8 = (f32[4,32,128]{2,1,0:T(8,128)S(1)}, f32[4,32,128]{2,1,0:T(8,128)S(1)}, u32[]{:S(2)}, u32[]{:S(2)}) collective-permute-start(f32[4,32,128]{2,1,0:T(8,128)S(1)} %get-tuple-element.92), channel_id=1, source_target_pairs={{0,2},{2,4},{4,6},{6,8},{8,10},{10,12},{12,14},{14,0},{1,3},{3,5},... | collective-permute-start | bytes 196616 | tf_op jit(solution)/shard_map/ppermute | solution.py:21
  33.8 6.4 %collective-permute-start.9 = (f32[4,32,128]{2,1,0:T(8,128)S(1)}, f32[4,32,128]{2,1,0:T(8,128)S(1)}, u32[]{:S(2)}, u32[]{:S(2)}) collective-permute-start(f32[4,32,128]{2,1,0:T(8,128)S(1)} %get-tuple-element.93), channel_id=1, source_target_pairs={{2,0},{4,2},{6,4},{8,6},{10,8},{12,10},{14,12},{0,14},{3,1},{5,3},... | collective-permute-start | bytes 196616 | tf_op jit(solution)/shard_map/ppermute | solution.py:24
  40.3 6.0 %collective-permute-start.10 = (f32[24,4,128]{2,1,0:T(4,128)S(1)}, f32[24,4,128]{2,1,0:T(4,128)S(1)}, u32[]{:S(2)}, u32[]{:S(2)}) collective-permute-start(f32[24,4,128]{2,1,0:T(4,128)S(1)} %get-tuple-element.84), channel_id=1, source_target_pairs={{0,1},{1,0},{2,3},{3,2},{4,5},{5,4},{6,7},{7,6},{8,9},{9,8},{10,11... | collective-permute-start | bytes 147464 | tf_op jit(solution)/shard_map/ppermute | solution.py:21
  41.3 4.9 %collective-permute-start.11 = (f32[24,4,128]{2,1,0:T(4,128)S(1)}, f32[24,4,128]{2,1,0:T(4,128)S(1)}, u32[]{:S(2)}, u32[]{:S(2)}) collective-permute-start(f32[24,4,128]{2,1,0:T(4,128)S(1)} %get-tuple-element.85), channel_id=1, source_target_pairs={{1,0},{0,1},{3,2},{2,3},{5,4},{4,5},{7,6},{6,7},{9,8},{8,9},{11,10... | collective-permute-start | bytes 147464 | tf_op jit(solution)/shard_map/ppermute | solution.py:24
  47.0 13.3 %copy-start = (f32[16,32,128]{2,1,0:T(8,128)}, f32[16,32,128]{2,1,0:T(8,128)S(1)}, u32[]{:S(2)}) copy-start(f32[16,32,128]{2,1,0:T(8,128)S(1)} %fusion.48) | copy-start | bytes 786436
  47.1 6.5 %collective-permute-start.12 = (f32[4,32,128]{2,1,0:T(8,128)S(1)}, f32[4,32,128]{2,1,0:T(8,128)S(1)}, u32[]{:S(2)}, u32[]{:S(2)}) collective-permute-start(f32[4,32,128]{2,1,0:T(8,128)S(1)} %get-tuple-element.90), channel_id=1, source_target_pairs={{0,2},{2,4},{4,6},{6,8},{8,10},{10,12},{12,14},{14,0},{1,3},{3,5},... | collective-permute-start | bytes 196616 | tf_op jit(solution)/shard_map/ppermute | solution.py:21
  47.1 6.4 %collective-permute-start.13 = (f32[4,32,128]{2,1,0:T(8,128)S(1)}, f32[4,32,128]{2,1,0:T(8,128)S(1)}, u32[]{:S(2)}, u32[]{:S(2)}) collective-permute-start(f32[4,32,128]{2,1,0:T(8,128)S(1)} %get-tuple-element.91), channel_id=1, source_target_pairs={{2,0},{4,2},{6,4},{8,6},{10,8},{12,10},{14,12},{0,14},{3,1},{5,3},... | collective-permute-start | bytes 196616 | tf_op jit(solution)/shard_map/ppermute | solution.py:24
  53.6 6.0 %collective-permute-start.14 = (f32[24,4,128]{2,1,0:T(4,128)S(1)}, f32[24,4,128]{2,1,0:T(4,128)S(1)}, u32[]{:S(2)}, u32[]{:S(2)}) collective-permute-start(f32[24,4,128]{2,1,0:T(4,128)S(1)} %get-tuple-element.82), channel_id=1, source_target_pairs={{0,1},{1,0},{2,3},{3,2},{4,5},{5,4},{6,7},{7,6},{8,9},{9,8},{10,11... | collective-permute-start | bytes 147464 | tf_op jit(solution)/shard_map/ppermute | solution.py:21
  54.6 4.9 %collective-permute-start.15 = (f32[24,4,128]{2,1,0:T(4,128)S(1)}, f32[24,4,128]{2,1,0:T(4,128)S(1)}, u32[]{:S(2)}, u32[]{:S(2)}) collective-permute-start(f32[24,4,128]{2,1,0:T(4,128)S(1)} %get-tuple-element.83), channel_id=1, source_target_pairs={{1,0},{0,1},{3,2},{2,3},{5,4},{4,5},{7,6},{6,7},{9,8},{8,9},{11,10... | collective-permute-start | bytes 147464 | tf_op jit(solution)/shard_map/ppermute | solution.py:24
  60.3 49.1 %copy-start.3 = (f32[16,32,128]{2,1,0:T(8,128)}, f32[16,32,128]{2,1,0:T(8,128)S(1)}, u32[]{:S(2)}) copy-start(f32[16,32,128]{2,1,0:T(8,128)S(1)} %fusion.67) | copy-start | bytes 786436
  60.5 48.4 %collective-permute-start.16 = (f32[4,16,32,128]{3,2,1,0:T(8,128)S(1)}, f32[4,16,32,128]{3,2,1,0:T(8,128)S(1)}, u32[]{:S(2)}, u32[]{:S(2)}) collective-permute-start(f32[4,16,32,128]{3,2,1,0:T(8,128)S(1)} %pad_maximum_fusion.1), channel_id=1, source_target_pairs={{0,8},{2,10},{4,12},{6,14},{8,0},{10,2},{12,4},{14,6},{1,9},{3,11}... | collective-permute-start | bytes 3145736 | tf_op jit(solution)/shard_map/ppermute | solution.py:32
  109.4 4.9 %copy-start.5 = (s32[32]{0:T(128)S(1)}, s32[32]{0:T(128)}, u32[]{:S(2)}) copy-start(s32[32]{0:T(128)} %param.26) | copy-start | bytes 388
  109.7 45.4 %collective-permute-start.17 = (f32[2,2,16,16,128]{4,3,2,1,0:T(8,128)S(1)}, f32[2,2,16,16,128]{4,3,2,1,0:T(8,128)S(1)}, u32[]{:S(2)}, u32[]{:S(2)}) collective-permute-start(f32[2,2,16,16,128]{4,3,2,1,0:T(8,128)S(1)} %get-tuple-element.80), channel_id=1, source_target_pairs={{0,1},{2,3},{4,5},{6,7},{8,9},{10,11},{12,13},{14,15},{16,17},{18,... | collective-permute-start | bytes 1572872 | tf_op jit(solution)/shard_map/ppermute | solution.py:21
  111.0 44.1 %collective-permute-start.18 = (f32[2,2,16,16,128]{4,3,2,1,0:T(8,128)S(1)}, f32[2,2,16,16,128]{4,3,2,1,0:T(8,128)S(1)}, u32[]{:S(2)}, u32[]{:S(2)}) collective-permute-start(f32[2,2,16,16,128]{4,3,2,1,0:T(8,128)S(1)} %get-tuple-element.81), channel_id=1, source_target_pairs={{1,0},{3,2},{5,4},{7,6},{9,8},{11,10},{13,12},{15,14},{17,16},{19,... | collective-permute-start | bytes 1572872 | tf_op jit(solution)/shard_map/ppermute | solution.py:24
  (5 other events, 11.0 us)
where the time goes:
time: 161 us; the launch traced here: 160 us
  waiting for transfers between devices  53.5 us (33%)
  between operations  42.5 us (26%)
  starting transfers between devices  29.1 us (18%)
  other arithmetic  27.9 us (17%)
  local copies, waits for them, and re-layouts  7.25 us (5%)
    ppermute x1, waiting for transfers between devices, from_behind(): return lax.ppermute(value, axis, pairs)  47.1 us
    ppermute x9, starting transfers between devices, extended(): lax.ppermute(lax.slice_in_dim(block, 0, width, axis=dim), axis, backward)  21.7 us
    scatter-add x4, other arithmetic, shards(): impulse.at[receiver_flat]  15.7 us
    ppermute x9, starting transfers between devices, extended(): lax.ppermute(lax.slice_in_dim(block, block.shape[dim] - width, None, axis...  7.31 us
    ppermute x9, waiting for transfers between devices, extended(): lax.ppermute(lax.slice_in_dim(block, block.shape[dim] - width, None, axis...  6.41 us
    scatter-add x4, other arithmetic, shards(): impulse.at[source_flat].add(jnp.where(source_live, wavelet[instant], 0.0))  4.12 us
  transfers between devices with their start and end apart: 19, of which 5 were waited for; matrix products, arithmetic and copies ran while one was open for 15% of the time, Pallas kernels for 0%

commit v1 on v0

v1 whole, which is shorter than its diff:
```python
import functools

import jax
import jax.numpy as jnp
from jax import lax
from jax.experimental import pallas as pl
from jax.experimental.pallas import tpu as pltpu
from jax.sharding import PartitionSpec as P

LAGS = 32
STEPS = 4
MARGIN = LAGS // 2
REACH = 4
CHUNKS = 4
STENCIL_WEIGHTS = (-205.0 / 72.0, 8.0 / 5.0, -1.0 / 5.0, 8.0 / 315.0, -1.0 / 560.0)
MESH = pl.DeviceIdType.MESH


def split_bf16(value):
    high = value.astype(jnp.bfloat16)
    low = (value - high.astype(jnp.float32)).astype(jnp.bfloat16)
    return high, low


def kernel(
    slabs,
    now_ref, before_ref, courant_ref, traces_ref, cells_ref, wavelet_ref, source_ref, offsets_ref,
    now_out, before_out, image_ref,
    p0, p1, p2, p3, p4, qa, qb0, qb1, qb2, qb3, impulse, partial,
    low_send, low_recv, high_send, high_recv, side_send, side_recv,
    pair_send, pair_recv, fwd_send, fwd_recv,
):
    depth, cols, along = now_ref.shape
    fields = [p0, p1, p2, p3, p4]
    qb = [qb0, qb1, qb2, qb3]
    part = depth // CHUNKS
    inner = pl.ds(MARGIN, cols)
    shot = lax.axis_index("shot")
    slab = lax.axis_index("slab")
    side = lax.axis_index("side")
    quarter = slabs // 4
    is_receiver = (slab < quarter) | (slab >= 3 * quarter)
    is_source = jnp.logical_not(is_receiver)
    has_low = (slab != quarter) & (slab != 3 * quarter)
    has_high = (slab != quarter - 1) & (slab != 3 * quarter - 1)
    low = (shot, lax.rem(slab + slabs - 1, slabs), side)
    high = (shot, lax.rem(slab + 1, slabs), side)
    partner = (shot, lax.rem(slab + 2 * quarter, slabs), side)
    peer = (shot, slab, 1 - side)

    def low_copy(step):
        return pltpu.make_async_remote_copy(
            src_ref=fields[step].at[pl.ds(REACH, REACH), inner],
            dst_ref=fields[step].at[pl.ds(REACH + depth, REACH), inner],
            send_sem=low_send.at[step], recv_sem=low_recv.at[step],
            device_id=low, device_id_type=MESH,
        )

    def high_copy(step):
        return pltpu.make_async_remote_copy(
            src_ref=fields[step].at[pl.ds(depth, REACH), inner],
            dst_ref=fields[step].at[pl.ds(0, REACH), inner],
            send_sem=high_send.at[step], recv_sem=high_recv.at[step],
            device_id=high, device_id_type=MESH,
        )

    side_from = pl.multiple_of(jnp.where(side == 0, cols, MARGIN), 8)
    side_to = pl.multiple_of(jnp.where(side == 0, 0, MARGIN + cols), 8)

    def side_copy(step):
        rows = pl.ds(REACH, depth)
        return pltpu.make_async_remote_copy(
            src_ref=fields[step].at[rows, pl.ds(side_from, MARGIN)],
            dst_ref=fields[step].at[rows, pl.ds(side_to, MARGIN)],
            send_sem=side_send.at[step], recv_sem=side_recv.at[step],
            device_id=peer, device_id_type=MESH,
        )

    def pair_copies(step, second):
        if not second:
            return [pltpu.make_async_remote_copy(
                src_ref=fields[step].at[pl.ds(REACH, depth), inner],
                dst_ref=qa.at[:, inner],
                send_sem=pair_send.at[CHUNKS], recv_sem=pair_recv.at[CHUNKS],
                device_id=partner, device_id_type=MESH,
            )]
        return [pltpu.make_async_remote_copy(
            src_ref=fields[step].at[pl.ds(REACH + c * part, part), inner],
            dst_ref=qb[c].at[:, inner],
            send_sem=pair_send.at[c], recv_sem=pair_recv.at[c],
            device_id=partner, device_id_type=MESH,
        ) for c in range(CHUNKS)]

    def forward(ref, index):
        return pltpu.make_async_remote_copy(
            src_ref=ref.at[:, pl.ds(side_from, MARGIN)],
            dst_ref=ref.at[:, pl.ds(side_to, MARGIN)],
            send_sem=fwd_send.at[index], recv_sem=fwd_recv.at[index],
            device_id=peer, device_id_type=MESH,
        )

    def clear(ref, pads):
        rows, width = ref.shape[0], ref.shape[1]

        def body(z, carry):
            ref[z, 0:MARGIN] = jnp.zeros((MARGIN, along), jnp.float32)
            ref[z, width - MARGIN : width] = jnp.zeros((MARGIN, along), jnp.float32)
            return carry

        lax.fori_loop(0, rows, body, 0)
        if pads:
            for z in list(range(REACH)) + list(range(rows - REACH, rows)):
                ref[z, inner] = jnp.zeros((cols, along), jnp.float32)

    def load_now(z, carry):
        p0[REACH + z, inner] = now_ref[z]
        return carry

    lax.fori_loop(0, depth, load_now, 0)
    for ref in fields:
        clear(ref, ref is not p4)
    for ref in [qa] + qb:
        clear(ref, False)

    barrier = pltpu.get_barrier_semaphore()
    pl.semaphore_signal(barrier, inc=1, device_id=peer, device_id_type=MESH)
    pl.semaphore_signal(barrier, inc=1, device_id=partner, device_id_type=MESH)

    @pl.when(has_low)
    def _():
        pl.semaphore_signal(barrier, inc=1, device_id=low, device_id_type=MESH)

    @pl.when(has_high)
    def _():
        pl.semaphore_signal(barrier, inc=1, device_id=high, device_id_type=MESH)

    pl.semaphore_wait(
        barrier, 2 + jnp.where(has_low, 1, 0) + jnp.where(has_high, 1, 0)
    )

    def start_depth(step):
        @pl.when(has_low)
        def _():
            low_copy(step).start()

        @pl.when(has_high)
        def _():
            high_copy(step).start()

    start_depth(0)
    side_copy(0).start()

    count = cells_ref.shape[1]
    first_lane = lax.broadcasted_iota(jnp.int32, (1, count), 1) == 0
    cells = jnp.where(
        is_receiver, cells_ref[...], jnp.where(first_lane, source_ref[0], -1)
    )
    depth_start = jnp.where(
        is_receiver, lax.rem(slab + quarter, slabs), slab - quarter
    ) * depth
    cols_all = 2 * cols
    safe = jnp.maximum(cells, 0)
    cell_depth = lax.div(safe, cols_all * along) - depth_start
    cell_across = lax.rem(lax.div(safe, along), cols_all) - side * cols
    cell_along = lax.rem(safe, along)
    inside = (
        (cells >= 0) & (cell_depth >= 0) & (cell_depth < depth)
        & (cell_across >= 0) & (cell_across < cols)
    )
    cell_row = jnp.where(inside, cell_depth * cols + cell_across, -1)
    row_hot = jnp.where(
        lax.broadcasted_iota(jnp.int32, (depth * cols, count), 0) == cell_row, 1.0, 0.0
    ).astype(jnp.bfloat16)
    along_hot = lax.broadcasted_iota(jnp.int32, (along, count), 0) == cell_along
    over_cells = (((1,), (1,)), ((), ()))
    for step in range(STEPS):
        amount = jnp.where(
            is_receiver,
            traces_ref[step : step + 1, :],
            jnp.where(first_lane, wavelet_ref[step], 0.0),
        )
        spread_high, spread_low = split_bf16(jnp.where(along_hot, amount, 0.0))
        both = lax.dot_general(
            row_hot, spread_high, over_cells, preferred_element_type=jnp.float32
        ) + lax.dot_general(
            row_hot, spread_low, over_cells, preferred_element_type=jnp.float32
        )
        impulse[step] = both.reshape(depth, cols, along)

    apart = jnp.abs(
        lax.broadcasted_iota(jnp.int32, (along, along), 0)
        - lax.broadcasted_iota(jnp.int32, (along, along), 1)
    )
    band = jnp.where(apart == 0, 3.0 * STENCIL_WEIGHTS[0], 0.0)
    for reach in range(1, REACH + 1):
        band = jnp.where(apart == reach, STENCIL_WEIGHTS[reach], band)
    band_high, band_low = split_bf16(band)

    def advance(step, first):
        field, later = fields[step], fields[step + 1]
        zs = pl.ds(first, part)
        centre = field[pl.ds(first + REACH, part), inner]
        c_high, c_low = split_bf16(centre.reshape(part * cols, along))
        summed = (
            jnp.dot(c_high, band_high, preferred_element_type=jnp.float32)
            + jnp.dot(c_low, band_high, preferred_element_type=jnp.float32)
            + jnp.dot(c_high, band_low, preferred_element_type=jnp.float32)
        ).reshape(part, cols, along)
        for reach in range(1, REACH + 1):
            pairs = (
                field[pl.ds(first + REACH + reach, part), inner]
                + field[pl.ds(first + REACH - reach, part), inner]
            ) + (
                field[pl.ds(first + REACH, part), MARGIN + reach : MARGIN + reach + cols]
                + field[pl.ds(first + REACH, part), MARGIN - reach : MARGIN - reach + cols]
            )
            summed = summed + STENCIL_WEIGHTS[reach] * pairs
        if step == 0:
            before = before_ref[zs]
        else:
            before = fields[step - 1][pl.ds(first + REACH, part), inner]
        result = 2.0 * centre - before + courant_ref[zs] * (summed + impulse[step, zs])
        later[pl.ds(first + REACH, part), inner] = result
        if step == STEPS - 1:
            now_out[zs] = result
            before_out[zs] = centre

    for step in range(STEPS):
        side_copy(step).wait_recv()

        def body(c, carry, step=step):
            advance(step, c * part)
            return carry

        lax.fori_loop(1, CHUNKS - 1, body, 0)

        @pl.when(has_high)
        def _():
            low_copy(step).wait_recv()

        @pl.when(has_low)
        def _():
            high_copy(step).wait_recv()

        def edge(c, carry, step=step):
            advance(step, c * (depth - part))
            return carry

        lax.fori_loop(0, 2, edge, 0)
        if step < STEPS - 1:
            start_depth(step + 1)
        side_copy(step + 1).start()

        @pl.when(is_source if step % 2 else is_receiver)
        def _():
            for copy in pair_copies(step + 1, step >= 2):
                copy.start()

    side_copy(STEPS).wait_recv()
    pair_copies(1, False)[0].wait_recv()
    forward(qa, CHUNKS).start()
    forward(qa, CHUNKS).wait_recv()
    slot_base = jnp.where(is_receiver, MARGIN, 0)
    sign = jnp.where(is_receiver, 1, -1)

    def starts(slot):
        lag = (offsets_ref[slot_base + slot] - MARGIN) * sign
        return MARGIN + lag, MARGIN - lag

    def first_product(own):
        def body(slot, carry):
            own_at, other_at = starts(slot)
            for z in range(depth):
                partial[z, slot] = (
                    own[REACH + z, pl.ds(own_at, cols)] * qa[z, pl.ds(other_at, cols)]
                )
            return carry

        lax.fori_loop(0, MARGIN, body, 0)

    def last_product(own, c):
        def body(slot, carry):
            own_at, other_at = starts(slot)
            for z in range(part):
                row = c * part + z
                image_ref[row, slot] = (
                    partial[row, slot]
                    + own[REACH + row, pl.ds(own_at, cols)]
                    * qb[c][z, pl.ds(other_at, cols)]
                ).astype(jnp.bfloat16)
            return carry

        lax.fori_loop(0, MARGIN, body, 0)

    @pl.when(is_source)
    def _():
        first_product(p4)

    @pl.when(is_receiver)
    def _():
        first_product(p3)

    seconds = pair_copies(3, True)
    seconds[0].wait_recv()
    forward(qb[0], 0).start()
    for c in range(CHUNKS):
        if c + 1 < CHUNKS:
            seconds[c + 1].wait_recv()
            forward(qb[c + 1], c + 1).start()
        forward(qb[c], c).wait_recv()

        @pl.when(is_source)
        def _():
            last_product(p2, c)

        @pl.when(is_receiver)
        def _():
            last_product(p1, c)

    for step in range(STEPS):
        @pl.when(has_low)
        def _():
            low_copy(step).wait_send()

        @pl.when(has_high)
        def _():
            high_copy(step).wait_send()

    for step in range(STEPS + 1):
        side_copy(step).wait_send()
    pair_copies(1, False)[0].wait_send()
    for c in range(CHUNKS):
        seconds[c].wait_send()
        forward(qb[c], c).wait_send()
    forward(qa, CHUNKS).wait_send()


def shards(field_now, field_before, courant, wavelet, source_cell, traces, receiver_cells, offsets):
    depth, cols, along = field_now.shape
    f32 = jnp.float32
    vmem = pl.BlockSpec(memory_space=pltpu.VMEM)
    smem = pl.BlockSpec(memory_space=pltpu.SMEM)
    field = pltpu.VMEM((depth + 2 * REACH, cols + 2 * MARGIN, along), f32)
    part = depth // CHUNKS
    dma = pltpu.SemaphoreType.DMA
    return pl.pallas_call(
        functools.partial(kernel, lax.axis_size("slab")),
        out_shape=(
            jax.ShapeDtypeStruct(field_now.shape, f32),
            jax.ShapeDtypeStruct(field_now.shape, f32),
            jax.ShapeDtypeStruct((depth, MARGIN, cols, along), jnp.bfloat16),
        ),
        in_specs=[vmem] * 5 + [smem] * 3,
        out_specs=(vmem, vmem, vmem),
        scratch_shapes=[field] * 5
        + [pltpu.VMEM((depth, cols + 2 * MARGIN, along), f32)]
        + [pltpu.VMEM((part, cols + 2 * MARGIN, along), f32)] * CHUNKS
        + [
            pltpu.VMEM((STEPS, depth, cols, along), f32),
            pltpu.VMEM((depth, MARGIN, cols, along), f32),
            dma((STEPS,)), dma((STEPS,)), dma((STEPS,)), dma((STEPS,)),
            dma((STEPS + 1,)), dma((STEPS + 1,)),
            dma((CHUNKS + 1,)), dma((CHUNKS + 1,)), dma((CHUNKS + 1,)), dma((CHUNKS + 1,)),
        ],
        compiler_params=pltpu.CompilerParams(
            collective_id=0, has_side_effects=True, vmem_limit_bytes=40 * 1024 * 1024
        ),
    )(
        field_now, field_before, courant, traces, receiver_cells.reshape(1, -1),
        wavelet, source_cell, offsets,
    )


def solution(mesh):
    return jax.shard_map(
        shards,
        mesh=mesh,
        in_specs=(
            P(("shot", "slab"), "side", None),
            P(("shot", "slab"), "side", None),
            P(("shot", "slab"), "side", None),
            P("shot"),
            P("shot"),
            P("shot", None),
            P("shot"),
            P("shot"),
        ),
        out_specs=(
            P(("shot", "slab"), "side", None),
            P(("shot", "slab"), "side", None),
            P(("shot", "slab"), None, "side", None),
        ),
        check_vma=False,
    )
```

time: 161 us -> 54.7 us (0.34)
  waiting for transfers between devices: 53.5 us -> 0 us
  Pallas kernels: 0 us -> 44.8 us
  between operations: 42.5 us -> 1.3 us
  starting transfers between devices: 29.1 us -> 0 us
  other arithmetic: 27.9 us -> 0 us
    ppermute x19 -> x0, waiting for transfers between devices: 53.5 us -> none  [the longest x1 47.1 us: from_behind(): return lax.ppermute(value, axis, pairs)]
    pallas_call x0 -> x1, Pallas kernels: none -> 44.8 us  [shards(): pl.pallas_call(functools.partial(kernel, lax.axis_size('slab')), out_shap...]
    ppermute x19 -> x0, starting transfers between devices: 29.1 us -> none  [the longest x9 21.7 us: extended(): lax.ppermute(lax.slice_in_dim(block, 0, width, axis=dim), axis, backward)]
    scatter-add x8 -> x0, other arithmetic: 19.8 us -> none  [the longest x4 15.7 us: shards(): impulse.at[receiver_flat]]
    unnamed x37 -> x17, local copies, waits for them, and re-layouts: 3.18 us -> 8.25 us
    reduce_sum x2 -> x0, other arithmetic: 2.9 us -> none  [shards(): slots.append(jnp.sum(s_piece * r_piece, axis=0).astype(jnp.bfloat16))]
    add x4 -> x0, other arithmetic: 2.46 us -> none  [shards(): later = 2.0 * now - before + courant * (stencil(padded) + impulse)]
    slice x7 -> x0, local copies, waits for them, and re-layouts: 2.04 us -> none  [the longest x1 0.88 us: extended(): lax.slice_in_dim(block, 0, width, axis=dim)]
  transfers between devices with their start and end apart: 19 -> 0, of which waited for: 5 -> 0; matrix products, arithmetic and copies ran while one was open for 15% -> 0% of each run, Pallas kernels for 0% -> 0%
where the time goes in v1:
time: 54.7 us; the launch traced here: 54.4 us
  Pallas kernels  44.8 us (82%)
  local copies, waits for them, and re-layouts  8.25 us (15%)
  between operations  1.3 us (2%)
    pallas_call x1, Pallas kernels, shards(): pl.pallas_call(functools.partial(kernel, lax.axis_size('slab')), out_shap...  44.8 us
    unnamed x17, local copies, waits for them, and re-layouts  8.25 us

profile of v1, /device:TPU:1, one launch (start us, length us, event | category | flops | bytes accessed | tf_op | source)
XLA Modules:
  0.0 54.4 jit_solution(11926932314220001449)
XLA Ops:
  1.3 0.0 copy-start
  1.3 0.9 %copy-done = f32[16,32,128]{2,1,0:T(8,128)S(1)} copy-done((f32[16,32,128]{2,1,0:T(8,128)S(1)}, f32[16,32,128]{2,1,0:T(8,128)}, u32[]{:S(2)}) %copy-start) | copy-done | bytes 262168
  2.2 0.0 copy-start.1
  2.2 0.9 %copy-done.1 = f32[16,32,128]{2,1,0:T(8,128)S(1)} copy-done((f32[16,32,128]{2,1,0:T(8,128)S(1)}, f32[16,32,128]{2,1,0:T(8,128)}, u32[]{:S(2)}) %copy-start.1) | copy-done | bytes 262168
  3.2 0.0 copy-start.2
  3.2 0.9 %copy-done.2 = f32[16,32,128]{2,1,0:T(8,128)S(1)} copy-done((f32[16,32,128]{2,1,0:T(8,128)S(1)}, f32[16,32,128]{2,1,0:T(8,128)}, u32[]{:S(2)}) %copy-start.2) | copy-done | bytes 262168
  4.1 0.0 copy-start.3
  4.1 0.7 %copy-done.3 = f32[4,512]{1,0:T(4,128)S(1)} copy-done((f32[4,512]{1,0:T(4,128)S(1)}, f32[4,512]{1,0:T(4,128)}, u32[]{:S(2)}) %copy-start.3) | copy-done | bytes 8216
  4.8 0.0 copy-start.4
  4.8 0.7 %copy-done.4 = s32[512]{0:T(512)S(1)} copy-done((s32[512]{0:T(512)S(1)}, s32[512]{0:T(512)}, u32[]{:S(2)}) %copy-start.4) | copy-done | bytes 2072
  5.5 0.0 copy-start.5
  5.5 0.7 %copy-done.5 = f32[4]{0:T(128)S(1)} copy-done((f32[4]{0:T(128)S(1)}, f32[4]{0:T(128)}, u32[]{:S(2)}) %copy-start.5) | copy-done | bytes 40
  6.2 0.0 copy-start.6
  6.2 0.7 %copy-done.6 = s32[32]{0:T(128)S(1)} copy-done((s32[32]{0:T(128)S(1)}, s32[32]{0:T(128)}, u32[]{:S(2)}) %copy-start.6) | copy-done | bytes 152
  6.8 44.8 %shard_map.103 = (f32[16,32,128]{2,1,0:T(8,128)S(1)}, f32[16,32,128]{2,1,0:T(8,128)S(1)}, bf16[16,16,32,128]{3,2,1,0:T(8,128)(2,1)S(1)}) custom-call(f32[16,32,128]{2,1,0:T(8,128)S(1)} %copy-done, f32[16,32,128]{2,1,0:T(8,128)S(1)} %copy-done.1, f32[16,32,128]{2,1,0:T(8,128)S(1)} %copy-done.2, f32[4,512]{1,0:T(4,128)S(1)} %copy-done.3, ...), custom_call_target="tpu_custom_call" | custom-call | tf_op jit(solution)/shard_map/pallas_call | solution.py:346
  51.7 0.7 %copy.15 = f32[16,32,128]{2,1,0:T(8,128)} copy(f32[16,32,128]{2,1,0:T(8,128)S(1)} %get-tuple-element.6) | data formatting | bytes 524288
  52.4 0.7 %copy.16 = f32[16,32,128]{2,1,0:T(8,128)} copy(f32[16,32,128]{2,1,0:T(8,128)S(1)} %get-tuple-element.7) | data formatting | bytes 524288
  53.1 1.3 %copy.17 = bf16[16,16,32,128]{3,2,1,0:T(8,128)(2,1)} copy(bf16[16,16,32,128]{3,2,1,0:T(8,128)(2,1)S(1)} %get-tuple-element.8) | data formatting | bytes 4194304
Async XLA Ops:
  1.3 1.0 %copy-start = (f32[16,32,128]{2,1,0:T(8,128)S(1)}, f32[16,32,128]{2,1,0:T(8,128)}, u32[]{:S(2)}) copy-start(f32[16,32,128]{2,1,0:T(8,128)} %now_ref.1) | copy-start | bytes 786436
  2.2 0.9 %copy-start.1 = (f32[16,32,128]{2,1,0:T(8,128)S(1)}, f32[16,32,128]{2,1,0:T(8,128)}, u32[]{:S(2)}) copy-start(f32[16,32,128]{2,1,0:T(8,128)} %before_ref.1) | copy-start | bytes 786436
  3.2 0.9 %copy-start.2 = (f32[16,32,128]{2,1,0:T(8,128)S(1)}, f32[16,32,128]{2,1,0:T(8,128)}, u32[]{:S(2)}) copy-start(f32[16,32,128]{2,1,0:T(8,128)} %courant_ref.1) | copy-start | bytes 786436
  4.1 0.7 %copy-start.3 = (f32[4,512]{1,0:T(4,128)S(1)}, f32[4,512]{1,0:T(4,128)}, u32[]{:S(2)}) copy-start(f32[4,512]{1,0:T(4,128)} %traces_ref.1) | copy-start | bytes 24580
  4.8 0.7 %copy-start.4 = (s32[512]{0:T(512)S(1)}, s32[512]{0:T(512)}, u32[]{:S(2)}) copy-start(s32[512]{0:T(512)} %param.14) | copy-start | bytes 6148
  5.5 0.7 %copy-start.5 = (f32[4]{0:T(128)S(1)}, f32[4]{0:T(128)}, u32[]{:S(2)}) copy-start(f32[4]{0:T(128)} %wavelet_ref.1) | copy-start | bytes 52
  6.2 0.7 %copy-start.6 = (s32[32]{0:T(128)S(1)}, s32[32]{0:T(128)}, u32[]{:S(2)}) copy-start(s32[32]{0:T(128)} %offsets_ref.1) | copy-start | bytes 388

commit v2 on v1

--- a/solution.py
+++ b/solution.py
@@ -24,13 +24,15 @@
 
 def kernel(
     slabs,
-    now_ref, before_ref, courant_ref, traces_ref, cells_ref, wavelet_ref, source_ref, offsets_ref,
-    now_out, before_out, image_ref,
+    now_hbm, before_hbm, courant_hbm, traces_hbm, cells_hbm, wavelet_hbm, source_hbm, offsets_hbm,
+    now_out, before_out, image_out,
     p0, p1, p2, p3, p4, qa, qb0, qb1, qb2, qb3, impulse, partial,
+    before_ref, courant_ref, traces_ref, cells_ref, wavelet_ref, source_ref, offsets_ref, load_sem,
+    image_ref, store_sem,
     low_send, low_recv, high_send, high_recv, side_send, side_recv,
     pair_send, pair_recv, fwd_send, fwd_recv,
 ):
-    depth, cols, along = now_ref.shape
+    depth, cols, along = now_hbm.shape
     fields = [p0, p1, p2, p3, p4]
     qb = [qb0, qb1, qb2, qb3]
     part = depth // CHUNKS
@@ -48,6 +50,18 @@
     partner = (shot, lax.rem(slab + 2 * quarter, slabs), side)
     peer = (shot, slab, 1 - side)
 
+    loads = [
+        pltpu.make_async_copy(source, target, load_sem.at[index])
+        for index, (source, target) in enumerate((
+            (now_hbm, p0.at[pl.ds(REACH, depth), inner]),
+            (cells_hbm, cells_ref), (traces_hbm, traces_ref),
+            (wavelet_hbm, wavelet_ref), (source_hbm, source_ref),
+            (before_hbm, before_ref), (courant_hbm, courant_ref), (offsets_hbm, offsets_ref),
+        ))
+    ]
+    for load in loads:
+        load.start()
+
     def low_copy(step):
         return pltpu.make_async_remote_copy(
             src_ref=fields[step].at[pl.ds(REACH, REACH), inner],
@@ -79,10 +93,12 @@
     def pair_copies(step, second):
         if not second:
             return [pltpu.make_async_remote_copy(
-                src_ref=fields[step].at[pl.ds(REACH, depth), inner],
-                dst_ref=qa.at[:, inner],
-                send_sem=pair_send.at[CHUNKS], recv_sem=pair_recv.at[CHUNKS],
+                src_ref=fields[step].at[pl.ds(REACH + first, rows), inner],
+                dst_ref=qa.at[pl.ds(first, rows), inner],
+                send_sem=pair_send.at[CHUNKS + index], recv_sem=pair_recv.at[CHUNKS + index],
                 device_id=partner, device_id_type=MESH,
+            ) for index, (first, rows) in enumerate(
+                ((part, depth - 2 * part), (0, part), (depth - part, part))
             )]
         return [pltpu.make_async_remote_copy(
             src_ref=fields[step].at[pl.ds(REACH + c * part, part), inner],
@@ -112,11 +128,6 @@
             for z in list(range(REACH)) + list(range(rows - REACH, rows)):
                 ref[z, inner] = jnp.zeros((cols, along), jnp.float32)
 
-    def load_now(z, carry):
-        p0[REACH + z, inner] = now_ref[z]
-        return carry
-
-    lax.fori_loop(0, depth, load_now, 0)
     for ref in fields:
         clear(ref, ref is not p4)
     for ref in [qa] + qb:
@@ -147,8 +158,12 @@
         def _():
             high_copy(step).start()
 
+    loads[0].wait()
     start_depth(0)
     side_copy(0).start()
+
+    for load in loads[1:5]:
+        load.wait()
 
     count = cells_ref.shape[1]
     first_lane = lax.broadcasted_iota(jnp.int32, (1, count), 1) == 0
@@ -173,19 +188,18 @@
     ).astype(jnp.bfloat16)
     along_hot = lax.broadcasted_iota(jnp.int32, (along, count), 0) == cell_along
     over_cells = (((1,), (1,)), ((), ()))
-    for step in range(STEPS):
+
+    def make_impulse(step):
         amount = jnp.where(
             is_receiver,
             traces_ref[step : step + 1, :],
             jnp.where(first_lane, wavelet_ref[step], 0.0),
         )
-        spread_high, spread_low = split_bf16(jnp.where(along_hot, amount, 0.0))
-        both = lax.dot_general(
-            row_hot, spread_high, over_cells, preferred_element_type=jnp.float32
-        ) + lax.dot_general(
-            row_hot, spread_low, over_cells, preferred_element_type=jnp.float32
-        )
-        impulse[step] = both.reshape(depth, cols, along)
+        spread = jnp.concatenate(split_bf16(jnp.where(along_hot, amount, 0.0)), axis=0)
+        both = lax.dot_general(row_hot, spread, over_cells, preferred_element_type=jnp.float32)
+        impulse[step] = (both[:, :along] + both[:, along:]).reshape(depth, cols, along)
+
+    make_impulse(0)
 
     apart = jnp.abs(
         lax.broadcasted_iota(jnp.int32, (along, along), 0)
@@ -221,10 +235,9 @@
             before = fields[step - 1][pl.ds(first + REACH, part), inner]
         result = 2.0 * centre - before + courant_ref[zs] * (summed + impulse[step, zs])
         later[pl.ds(first + REACH, part), inner] = result
-        if step == STEPS - 1:
-            now_out[zs] = result
-            before_out[zs] = centre
-
+
+    for load in loads[5:]:
+        load.wait()
     for step in range(STEPS):
         side_copy(step).wait_recv()
 
@@ -233,6 +246,13 @@
             return carry
 
         lax.fori_loop(1, CHUNKS - 1, body, 0)
+
+        sends_pair = is_source if step % 2 else is_receiver
+        copies = pair_copies(step + 1, step >= 2)
+        if step < 2:
+            @pl.when(sends_pair)
+            def _():
+                copies[0].start()
 
         @pl.when(has_high)
         def _():
@@ -251,13 +271,26 @@
             start_depth(step + 1)
         side_copy(step + 1).start()
 
-        @pl.when(is_source if step % 2 else is_receiver)
-        def _():
-            for copy in pair_copies(step + 1, step >= 2):
+        @pl.when(sends_pair)
+        def _():
+            for copy in copies[1:] if step < 2 else copies:
                 copy.start()
 
+        if step == 0:
+            for later_step in range(1, STEPS):
+                make_impulse(later_step)
+
+    stores = [
+        pltpu.make_async_copy(
+            ref.at[pl.ds(REACH, depth), inner], target, store_sem.at[CHUNKS + index]
+        )
+        for index, (ref, target) in enumerate(((p4, now_out), (p3, before_out)))
+    ]
+    for store in stores:
+        store.start()
     side_copy(STEPS).wait_recv()
-    pair_copies(1, False)[0].wait_recv()
+    for copy in pair_copies(1, False):
+        copy.wait_recv()
     forward(qa, CHUNKS).start()
     forward(qa, CHUNKS).wait_recv()
     slot_base = jnp.where(is_receiver, MARGIN, 0)
@@ -317,6 +350,14 @@
         def _():
             last_product(p1, c)
 
+        rows = pl.ds(c * part, part)
+        stores.append(
+            pltpu.make_async_copy(image_ref.at[rows], image_out.at[rows], store_sem.at[c])
+        )
+        stores[-1].start()
+
+    for store in stores:
+        store.wait()
     for step in range(STEPS):
         @pl.when(has_low)
         def _():
@@ -328,7 +369,8 @@
 
     for step in range(STEPS + 1):
         side_copy(step).wait_send()
-    pair_copies(1, False)[0].wait_send()
+    for copy in pair_copies(1, False):
+        copy.wait_send()
     for c in range(CHUNKS):
         seconds[c].wait_send()
         forward(qb[c], c).wait_send()
@@ -338,8 +380,8 @@
 def shards(field_now, field_before, courant, wavelet, source_cell, traces, receiver_cells, offsets):
     depth, cols, along = field_now.shape
     f32 = jnp.float32
-    vmem = pl.BlockSpec(memory_space=pltpu.VMEM)
-    smem = pl.BlockSpec(memory_space=pltpu.SMEM)
+    hbm = pl.BlockSpec(memory_space=pltpu.HBM)
+    i32 = jnp.int32
     field = pltpu.VMEM((depth + 2 * REACH, cols + 2 * MARGIN, along), f32)
     part = depth // CHUNKS
     dma = pltpu.SemaphoreType.DMA
@@ -350,20 +392,25 @@
             jax.ShapeDtypeStruct(field_now.shape, f32),
             jax.ShapeDtypeStruct((depth, MARGIN, cols, along), jnp.bfloat16),
         ),
-        in_specs=[vmem] * 5 + [smem] * 3,
-        out_specs=(vmem, vmem, vmem),
+        in_specs=[hbm] * 8,
+        out_specs=(hbm, hbm, hbm),
         scratch_shapes=[field] * 5
         + [pltpu.VMEM((depth, cols + 2 * MARGIN, along), f32)]
         + [pltpu.VMEM((part, cols + 2 * MARGIN, along), f32)] * CHUNKS
         + [
             pltpu.VMEM((STEPS, depth, cols, along), f32),
             pltpu.VMEM((depth, MARGIN, cols, along), f32),
+            pltpu.VMEM(field_now.shape, f32), pltpu.VMEM(field_now.shape, f32),
+            pltpu.VMEM(traces.shape, f32), pltpu.VMEM((1, receiver_cells.shape[0]), i32),
+            pltpu.SMEM(wavelet.shape, f32), pltpu.SMEM(source_cell.shape, i32),
+            pltpu.SMEM(offsets.shape, i32), dma((8,)),
+            pltpu.VMEM((depth, MARGIN, cols, along), jnp.bfloat16), dma((CHUNKS + 2,)),
             dma((STEPS,)), dma((STEPS,)), dma((STEPS,)), dma((STEPS,)),
             dma((STEPS + 1,)), dma((STEPS + 1,)),
-            dma((CHUNKS + 1,)), dma((CHUNKS + 1,)), dma((CHUNKS + 1,)), dma((CHUNKS + 1,)),
+            dma((CHUNKS + 3,)), dma((CHUNKS + 3,)), dma((CHUNKS + 1,)), dma((CHUNKS + 1,)),
         ],
         compiler_params=pltpu.CompilerParams(
-            collective_id=0, has_side_effects=True, vmem_limit_bytes=40 * 1024 * 1024
+            collective_id=0, has_side_effects=True, vmem_limit_bytes=61 * 1024 * 1024
         ),
     )(
         field_now, field_before, courant, traces, receiver_cells.reshape(1, -1),

time: 54.7 us -> 49.1 us (0.90)
  Pallas kernels: 44.8 us -> 40.9 us
  local copies, waits for them, and re-layouts: 8.25 us -> 6.71 us
    pallas_call x1, Pallas kernels: 44.8 us -> 40.9 us  [shards(): pl.pallas_call(functools.partial(kernel, lax.axis_size('slab')), out_shap...]
    unnamed x17 -> x3, local copies, waits for them, and re-layouts: 8.25 us -> 6.71 us
where the time goes in v2:
time: 49.1 us; the launch traced here: 48.9 us
  Pallas kernels  40.9 us (83%)
  local copies, waits for them, and re-layouts  6.71 us (14%)
  between operations  1.29 us (3%)
    pallas_call x1, Pallas kernels, shards(): pl.pallas_call(functools.partial(kernel, lax.axis_size('slab')), out_shap...  40.9 us
    unnamed x3, local copies, waits for them, and re-layouts  6.71 us

profile of v2, /device:TPU:1, one launch (start us, length us, event | category | flops | bytes accessed | tf_op | source)
XLA Modules:
  0.0 48.9 jit_solution(11254995055206756008)
XLA Ops:
  1.3 40.9 %shard_map.103 = (f32[16,32,128]{2,1,0:T(8,128)}, f32[16,32,128]{2,1,0:T(8,128)}, bf16[16,16,32,128]{3,2,1,0:T(8,128)(2,1)}) custom-call(f32[16,32,128]{2,1,0:T(8,128)} %now_hbm.1, f32[16,32,128]{2,1,0:T(8,128)} %before_hbm.1, f32[16,32,128]{2,1,0:T(8,128)} %courant_hbm.1, f32[4,512]{1,0:T(4,128)} %traces_hbm.1, s32[1,512]{1,0:T(1,128)} %bitcast.1, ...), custom_call_target="tpu_custom_call" | custom-call | tf_op jit(solution)/shard_map/pallas_call | solution.py:388
  42.2 1.7 %copy.15 = f32[16,32,128]{2,1,0:T(8,128)} copy(f32[16,32,128]{2,1,0:T(8,128)} %get-tuple-element.6) | data formatting | bytes 524288
  43.9 1.7 %copy.16 = f32[16,32,128]{2,1,0:T(8,128)} copy(f32[16,32,128]{2,1,0:T(8,128)} %get-tuple-element.7) | data formatting | bytes 524288
  45.5 3.4 %copy.17 = bf16[16,16,32,128]{3,2,1,0:T(8,128)(2,1)} copy(bf16[16,16,32,128]{3,2,1,0:T(8,128)(2,1)} %get-tuple-element.8) | data formatting | bytes 4194304

commit v3 on v2

--- a/solution.py
+++ b/solution.py
@@ -377,15 +377,37 @@
     forward(qa, CHUNKS).wait_send()
 
 
+def store_kernel(now_in, before_in, image_in, now_out, before_out, image_out, sem):
+    depth = now_in.shape[0]
+    pieces = []
+    for source, target, count in (
+        (image_in, image_out, 8), (now_in, now_out, 2), (before_in, before_out, 2),
+    ):
+        rows = depth // count
+        pieces += [
+            (source.at[pl.ds(k * rows, rows)], target.at[pl.ds(k * rows, rows)])
+            for k in range(count)
+        ]
+    copies = [
+        pltpu.make_async_copy(source, target, sem.at[index])
+        for index, (source, target) in enumerate(pieces)
+    ]
+    for copy in copies:
+        copy.start()
+    for copy in copies:
+        copy.wait()
+
+
 def shards(field_now, field_before, courant, wavelet, source_cell, traces, receiver_cells, offsets):
     depth, cols, along = field_now.shape
     f32 = jnp.float32
     hbm = pl.BlockSpec(memory_space=pltpu.HBM)
+    anywhere = pl.BlockSpec(memory_space=pl.ANY)
     i32 = jnp.int32
     field = pltpu.VMEM((depth + 2 * REACH, cols + 2 * MARGIN, along), f32)
     part = depth // CHUNKS
     dma = pltpu.SemaphoreType.DMA
-    return pl.pallas_call(
+    results = pl.pallas_call(
         functools.partial(kernel, lax.axis_size("slab")),
         out_shape=(
             jax.ShapeDtypeStruct(field_now.shape, f32),
@@ -393,7 +415,7 @@
             jax.ShapeDtypeStruct((depth, MARGIN, cols, along), jnp.bfloat16),
         ),
         in_specs=[hbm] * 8,
-        out_specs=(hbm, hbm, hbm),
+        out_specs=(anywhere, anywhere, anywhere),
         scratch_shapes=[field] * 5
         + [pltpu.VMEM((depth, cols + 2 * MARGIN, along), f32)]
         + [pltpu.VMEM((part, cols + 2 * MARGIN, along), f32)] * CHUNKS
@@ -416,6 +438,14 @@
         field_now, field_before, courant, traces, receiver_cells.reshape(1, -1),
         wavelet, source_cell, offsets,
     )
+    return pl.pallas_call(
+        store_kernel,
+        out_shape=tuple(jax.ShapeDtypeStruct(r.shape, r.dtype) for r in results),
+        in_specs=[anywhere] * 3,
+        out_specs=(hbm, hbm, hbm),
+        scratch_shapes=[dma((12,))],
+        compiler_params=pltpu.CompilerParams(vmem_limit_bytes=61 * 1024 * 1024),
+    )(*results)
 
 
 def solution(mesh):

time: 49.1 us -> 123 us (2.51)
  Pallas kernels: 40.9 us -> 122 us
  local copies, waits for them, and re-layouts: 6.71 us -> 0 us
    pallas_call x0 -> x1, Pallas kernels: none -> 80.6 us  [shards(): pl.pallas_call(store_kernel, out_shape=tuple((jax.ShapeDtypeStruct(r.shap...]
    unnamed x3 -> x0, local copies, waits for them, and re-layouts: 6.71 us -> none
where the time goes in v3:
time: 123 us
  Pallas kernels  122 us (99%)
  between operations  1.29 us (1%)
    pallas_call x1, Pallas kernels, shards(): pl.pallas_call(store_kernel, out_shape=tuple((jax.ShapeDtypeStruct(r.shap...  80.6 us
    pallas_call x1, Pallas kernels, shards(): pl.pallas_call(functools.partial(kernel, lax.axis_size('slab')), out_shap...  40.9 us

profile of v3, /device:TPU:1, one launch (start us, length us, event | category | flops | bytes accessed | tf_op | source)
XLA Modules:
  0.0 122.8 jit_solution(736015541227490525)
XLA Ops:
  1.3 40.9 %shard_map.103 = (f32[16,32,128]{2,1,0:T(8,128)}, f32[16,32,128]{2,1,0:T(8,128)}, bf16[16,16,32,128]{3,2,1,0:T(8,128)(2,1)}) custom-call(f32[16,32,128]{2,1,0:T(8,128)} %now_hbm.1, f32[16,32,128]{2,1,0:T(8,128)} %before_hbm.1, f32[16,32,128]{2,1,0:T(8,128)} %courant_hbm.1, f32[4,512]{1,0:T(4,128)} %traces_hbm.1, s32[1,512]{1,0:T(1,128)} %bitcast.1, ...), custom_call_target="tpu_custom_call" | custom-call | tf_op jit(solution)/shard_map/pallas_call | solution.py:410
  42.2 80.6 %shard_map.104 = (f32[16,32,128]{2,1,0:T(8,128)}, f32[16,32,128]{2,1,0:T(8,128)}, bf16[16,16,32,128]{3,2,1,0:T(8,128)(2,1)}) custom-call(f32[16,32,128]{2,1,0:T(8,128)} %get-tuple-element.6.now_in, f32[16,32,128]{2,1,0:T(8,128)} %get-tuple-element.7.before_in, bf16[16,16,32,128]{3,2,1,0:T(8,128)(2,1)} %get-tuple-element.8.image_in), custom_call_target="tpu_custom_call" | custom-call | tf_op jit(solution)/shard_map/pallas_call | solution.py:441

commit v4 on v2

--- a/solution.py
+++ b/solution.py
@@ -377,15 +377,46 @@
     forward(qa, CHUNKS).wait_send()
 
 
+def store_kernel(
+    now_in, before_in, image_in, now_out, before_out, image_out,
+    now_held, before_held, image_held, in_sem, out_sem,
+):
+    depth = now_in.shape[0]
+    fetches, stores = [], []
+    for source, held, target, count in (
+        (image_in, image_held, image_out, 4),
+        (now_in, now_held, now_out, 1),
+        (before_in, before_held, before_out, 1),
+    ):
+        rows = depth // count
+        for k in range(count):
+            piece = pl.ds(k * rows, rows)
+            index = len(fetches)
+            fetches.append(
+                pltpu.make_async_copy(source.at[piece], held.at[piece], in_sem.at[index])
+            )
+            stores.append(
+                pltpu.make_async_copy(held.at[piece], target.at[piece], out_sem.at[index])
+            )
+    for fetch in fetches:
+        fetch.start()
+    for fetch, store in zip(fetches, stores):
+        fetch.wait()
+        store.start()
+    for store in stores:
+        store.wait()
+
+
 def shards(field_now, field_before, courant, wavelet, source_cell, traces, receiver_cells, offsets):
     depth, cols, along = field_now.shape
     f32 = jnp.float32
     hbm = pl.BlockSpec(memory_space=pltpu.HBM)
+    anywhere = pl.BlockSpec(memory_space=pl.ANY)
     i32 = jnp.int32
     field = pltpu.VMEM((depth + 2 * REACH, cols + 2 * MARGIN, along), f32)
     part = depth // CHUNKS
     dma = pltpu.SemaphoreType.DMA
-    return pl.pallas_call(
+    results = pl.pallas_call(
         functools.partial(kernel, lax.axis_size("slab")),
         out_shape=(
             jax.ShapeDtypeStruct(field_now.shape, f32),
@@ -393,7 +424,7 @@
             jax.ShapeDtypeStruct((depth, MARGIN, cols, along), jnp.bfloat16),
         ),
         in_specs=[hbm] * 8,
-        out_specs=(hbm, hbm, hbm),
+        out_specs=(anywhere, anywhere, anywhere),
         scratch_shapes=[field] * 5
         + [pltpu.VMEM((depth, cols + 2 * MARGIN, along), f32)]
         + [pltpu.VMEM((part, cols + 2 * MARGIN, along), f32)] * CHUNKS
@@ -416,6 +447,14 @@
         field_now, field_before, courant, traces, receiver_cells.reshape(1, -1),
         wavelet, source_cell, offsets,
     )
+    return pl.pallas_call(
+        store_kernel,
+        out_shape=tuple(jax.ShapeDtypeStruct(r.shape, r.dtype) for r in results),
+        in_specs=[anywhere] * 3,
+        out_specs=(hbm, hbm, hbm),
+        scratch_shapes=[pltpu.VMEM(r.shape, r.dtype) for r in results] + [dma((6,)), dma((6,))],
+        compiler_params=pltpu.CompilerParams(vmem_limit_bytes=61 * 1024 * 1024),
+    )(*results)
 
 
 def solution(mesh):

time: 49.1 us -> 45 us (0.916)
  local copies, waits for them, and re-layouts: 6.71 us -> 0 us
  Pallas kernels: 40.9 us -> 43.5 us
    unnamed x3 -> x0, local copies, waits for them, and re-layouts: 6.71 us -> none
    pallas_call x0 -> x1, Pallas kernels: none -> 2.63 us  [shards(): pl.pallas_call(store_kernel, out_shape=tuple((jax.ShapeDtypeStruct(r.shap...]
where the time goes in v4:
time: 45 us; the launch traced here: 44.8 us
  Pallas kernels  43.5 us (97%)
  between operations  1.29 us (3%)
    pallas_call x1, Pallas kernels, shards(): pl.pallas_call(functools.partial(kernel, lax.axis_size('slab')), out_shap...  40.9 us
    pallas_call x1, Pallas kernels, shards(): pl.pallas_call(store_kernel, out_shape=tuple((jax.ShapeDtypeStruct(r.shap...  2.63 us

profile of v4, /device:TPU:1, one launch (start us, length us, event | category | flops | bytes accessed | tf_op | source)
XLA Modules:
  0.0 44.8 jit_solution(3947736710997378017)
XLA Ops:
  1.3 40.9 %shard_map.103 = (f32[16,32,128]{2,1,0:T(8,128)}, f32[16,32,128]{2,1,0:T(8,128)}, bf16[16,16,32,128]{3,2,1,0:T(8,128)(2,1)}) custom-call(f32[16,32,128]{2,1,0:T(8,128)} %now_hbm.1, f32[16,32,128]{2,1,0:T(8,128)} %before_hbm.1, f32[16,32,128]{2,1,0:T(8,128)} %courant_hbm.1, f32[4,512]{1,0:T(4,128)} %traces_hbm.1, s32[1,512]{1,0:T(1,128)} %bitcast.1, ...), custom_call_target="tpu_custom_call" | custom-call | tf_op jit(solution)/shard_map/pallas_call | solution.py:419
  42.2 2.6 %shard_map.104 = (f32[16,32,128]{2,1,0:T(8,128)}, f32[16,32,128]{2,1,0:T(8,128)}, bf16[16,16,32,128]{3,2,1,0:T(8,128)(2,1)}) custom-call(f32[16,32,128]{2,1,0:T(8,128)} %get-tuple-element.6.now_in, f32[16,32,128]{2,1,0:T(8,128)} %get-tuple-element.7.before_in, bf16[16,16,32,128]{3,2,1,0:T(8,128)(2,1)} %get-tuple-element.8.image_in), custom_call_target="tpu_custom_call" | custom-call | tf_op jit(solution)/shard_map/pallas_call | solution.py:450

commit v5 on v4

--- a/solution.py
+++ b/solution.py
@@ -249,10 +249,13 @@
 
         sends_pair = is_source if step % 2 else is_receiver
         copies = pair_copies(step + 1, step >= 2)
-        if step < 2:
-            @pl.when(sends_pair)
-            def _():
-                copies[0].start()
+        early = copies[:1] if step < 2 else copies[1:-1]
+        late = copies[1:] if step < 2 else [copies[0], copies[-1]]
+
+        @pl.when(sends_pair)
+        def _():
+            for copy in early:
+                copy.start()
 
         @pl.when(has_high)
         def _():
@@ -273,7 +276,7 @@
 
         @pl.when(sends_pair)
         def _():
-            for copy in copies[1:] if step < 2 else copies:
+            for copy in late:
                 copy.start()
 
         if step == 0:
@@ -334,12 +337,14 @@
         first_product(p3)
 
     seconds = pair_copies(3, True)
-    seconds[0].wait_recv()
-    forward(qb[0], 0).start()
-    for c in range(CHUNKS):
-        if c + 1 < CHUNKS:
-            seconds[c + 1].wait_recv()
-            forward(qb[c + 1], c + 1).start()
+    order = list(range(1, CHUNKS - 1)) + [0, CHUNKS - 1]
+    seconds[order[0]].wait_recv()
+    forward(qb[order[0]], order[0]).start()
+    for place, c in enumerate(order):
+        if place + 1 < CHUNKS:
+            after = order[place + 1]
+            seconds[after].wait_recv()
+            forward(qb[after], after).start()
         forward(qb[c], c).wait_recv()
 
         @pl.when(is_source)

time: 45 us -> 43.2 us (0.960)
  Pallas kernels: 43.5 us -> 41.8 us
    pallas_call x1, Pallas kernels: 40.9 us -> 39.2 us  [shards(): pl.pallas_call(functools.partial(kernel, lax.axis_size('slab')), out_shap...]
where the time goes in v5:
time: 43.2 us; the launch traced here: 43.1 us
  Pallas kernels  41.8 us (97%)
  between operations  1.29 us (3%)
    pallas_call x1, Pallas kernels, shards(): pl.pallas_call(functools.partial(kernel, lax.axis_size('slab')), out_shap...  39.2 us
    pallas_call x1, Pallas kernels, shards(): pl.pallas_call(store_kernel, out_shape=tuple((jax.ShapeDtypeStruct(r.shap...  2.63 us

profile of v5, /device:TPU:1, one launch (start us, length us, event | category | flops | bytes accessed | tf_op | source)
XLA Modules:
  0.0 43.1 jit_solution(6938607417280003575)
XLA Ops:
  1.3 39.2 %shard_map.103 = (f32[16,32,128]{2,1,0:T(8,128)}, f32[16,32,128]{2,1,0:T(8,128)}, bf16[16,16,32,128]{3,2,1,0:T(8,128)(2,1)}) custom-call(f32[16,32,128]{2,1,0:T(8,128)} %now_hbm.1, f32[16,32,128]{2,1,0:T(8,128)} %before_hbm.1, f32[16,32,128]{2,1,0:T(8,128)} %courant_hbm.1, f32[4,512]{1,0:T(4,128)} %traces_hbm.1, s32[1,512]{1,0:T(1,128)} %bitcast.1, ...), custom_call_target="tpu_custom_call" | custom-call | tf_op jit(solution)/shard_map/pallas_call | solution.py:424
  40.4 2.6 %shard_map.104 = (f32[16,32,128]{2,1,0:T(8,128)}, f32[16,32,128]{2,1,0:T(8,128)}, bf16[16,16,32,128]{3,2,1,0:T(8,128)(2,1)}) custom-call(f32[16,32,128]{2,1,0:T(8,128)} %get-tuple-element.6.now_in, f32[16,32,128]{2,1,0:T(8,128)} %get-tuple-element.7.before_in, bf16[16,16,32,128]{3,2,1,0:T(8,128)(2,1)} %get-tuple-element.8.image_in), custom_call_target="tpu_custom_call" | custom-call | tf_op jit(solution)/shard_map/pallas_call | solution.py:455
